TPU v7x, 32 devices: a whole 2x2x4 slice. The times are simulated.
32 devices in a mesh: blocks: 2 (over x), depth: 4 (over y, core), angle: 4 (over z).
Axes of the slice: x: 2, y: 2, z: 4, core: 2. Of those that a mesh axis runs over, the one named last changes fastest.
Arguments:
- index_change: float32 [16, 256, 256], P(('blocks', 'depth')), parts along dimension 0, may hold values from -4 to 4
- measured: float32 [16, 256, 256], P(('blocks', 'angle')), parts along dimension 0, may hold values from 0.25 to 2
- angle_index: int32 [16, 2], P(('blocks', 'angle')), parts along dimension 0, may hold values from -25 to 25
- cutoff: int32 [1], replicated, may hold values from 32 to 128
Outputs:
- gradient: float32 [16, 256, 256], P(('blocks', 'depth'), 'angle'), parts along dimension 0
There are 2 independent parts, one for each index of `blocks`. A program takes and returns all parts, laid end to end along the dimension named above; an argument that names none is the same for every part. Nothing has to cross between parts.
All inputs are finite; a program needn't handle non-finite values.
Results may differ from a plain program's by a relative error of at most 0.0003.
Values sent between devices are 32-bit elements; how exact they have to be, the bound alone decides.
A program may use at most 64 MiB of HBM per device.

v0:
```python
import math

import jax
import jax.numpy as jnp
from jax import lax
from jax.sharding import PartitionSpec as P

highest = lax.Precision.HIGHEST
screen_scale = 0.25


def passed_along(shard, axis, by):
    size = lax.axis_size(axis)
    pairs = [(i, i + by) for i in range(size) if 0 <= i + by < size]
    return lax.ppermute(shard, axis, pairs)


def dft_tables(width):
    index = jnp.arange(width, dtype=jnp.int32)
    angles = 2.0 * math.pi / width * (index[:, None] * index[None, :] % width).astype(jnp.float32)
    cosine = jnp.cos(angles)
    sine = jnp.sin(angles)
    forward_big = jnp.concatenate(
        [jnp.concatenate([cosine, sine], 1), jnp.concatenate([-sine, cosine], 1)], 0
    )
    inverse_big = (
        jnp.concatenate(
            [jnp.concatenate([cosine, -sine], 1), jnp.concatenate([sine, cosine], 1)], 0
        )
        / width
    )
    return ((forward_big, cosine, -sine), (inverse_big, cosine / width, sine / width))


def transform(field, table):
    big, part_re, part_im = table
    width = field.shape[1]
    left = jnp.dot(big, field.reshape(2 * width, width), precision=highest)
    real_part = jnp.dot(left, part_re, precision=highest)
    imag_part = jnp.dot(left, part_im, precision=highest)
    return jnp.stack([real_part[:width] - imag_part[width:], imag_part[:width] + real_part[width:]])


def complex_mul(field, mult_re, mult_im):
    return jnp.stack(
        [field[0] * mult_re - field[1] * mult_im, field[0] * mult_im + field[1] * mult_re]
    )


def body(index_change, measured, angle_index, cutoff):
    slabs = index_change.shape[0]
    width = index_change.shape[1]
    members = measured.shape[0]
    levels = lax.axis_size("depth")
    place = lax.axis_index("depth")
    forward_table, inverse_table = dft_tables(width)
    index = jnp.arange(width, dtype=jnp.int32)
    freq = (index + width // 2) % width - width // 2
    frequency_sq = freq[:, None] * freq[:, None] + freq[None, :] * freq[None, :]
    phi = (
        13.0
        / width
        * (jnp.sqrt(0.64 * width * width - frequency_sq.astype(jnp.float32)) - 0.8 * width)
    )
    prop_re = jnp.cos(phi)
    prop_im = jnp.sin(phi)
    pupil = (frequency_sq <= cutoff[0] * cutoff[0]).astype(jnp.float32)
    screen_re = jnp.cos(screen_scale * index_change)
    screen_im = jnp.sin(screen_scale * index_change)

    def filtered(field, mult_re, mult_im):
        return transform(
            complex_mul(transform(field, forward_table), mult_re, mult_im), inverse_table
        )

    def pupil_filter(field):
        return transform(transform(field, forward_table) * pupil, inverse_table)

    def incident(member):
        pair = lax.dynamic_index_in_dim(angle_index, member, 0, keepdims=False)
        phase = (
            2.0
            * math.pi
            / width
            * ((pair[0] * index[:, None] + pair[1] * index[None, :]) % width).astype(jnp.float32)
        )
        return jnp.stack([jnp.cos(phase), jnp.sin(phase)])

    def slab_down(field):
        fields = []
        for slice_index in range(slabs):
            field = complex_mul(
                filtered(field, prop_re, prop_im), screen_re[slice_index], screen_im[slice_index]
            )
            fields.append(field)
        return (field, jnp.stack(fields))

    def forward_step(moment, state):
        incoming, stored = state
        member = moment - place
        active = (member >= 0) & (member < members)
        member = jnp.clip(member, 0, members - 1)
        start = jnp.where(place == 0, incident(member), incoming)

        def forward_active_case(operands):
            last, fields = slab_down(operands[0])
            return (last, lax.dynamic_update_index_in_dim(operands[1], fields, member, 0))

        def forward_spare_case(operands):
            return (jnp.zeros_like(operands[0]), operands[1])

        outgoing, stored = lax.cond(
            active, forward_active_case, forward_spare_case, (start, stored)
        )
        incoming = passed_along(outgoing, "depth", 1)
        return (incoming, stored)

    def top_adjoint(bottom, member):
        image = pupil_filter(bottom)
        target = lax.dynamic_index_in_dim(measured, member, 0, keepdims=False)
        misfit = image[0] * image[0] + image[1] * image[1] - target
        return pupil_filter(2.0 * misfit * image)

    def slab_up(adjoint, total, member, stored):
        kept = lax.dynamic_index_in_dim(stored, member, 0, keepdims=False)
        field = kept[slabs - 1]
        terms = [None] * slabs
        for slice_index in reversed(range(slabs)):
            field = kept[slice_index]
            terms[slice_index] = screen_scale * (field[0] * adjoint[1] - field[1] * adjoint[0])
            adjoint = filtered(
                complex_mul(adjoint, screen_re[slice_index], -screen_im[slice_index]),
                prop_re,
                -prop_im,
            )
        return (adjoint, total + jnp.stack(terms))

    def adjoint_step(moment, state, stored):
        incoming, total = state
        member = moment - (levels - 1 - place)
        active = (member >= 0) & (member < members)
        member = jnp.clip(member, 0, members - 1)

        def adjoint_active_case(operands):
            kept = lax.dynamic_index_in_dim(stored, member, 0, keepdims=False)
            bottom = kept[slabs - 1]
            start = lax.cond(
                place == levels - 1, lambda: top_adjoint(bottom, member), lambda: operands[0]
            )
            return slab_up(start, operands[1], member, stored)

        def adjoint_spare_case(operands):
            return (jnp.zeros_like(operands[0]), operands[1])

        outgoing, total = lax.cond(
            active, adjoint_active_case, adjoint_spare_case, (incoming, total)
        )
        incoming = passed_along(outgoing, "depth", -1)
        return (incoming, total)

    zero_field = jnp.zeros((2, width, width), jnp.float32)
    stored_start = jnp.zeros((members, slabs, 2, width, width), jnp.float32)
    forward_state = (zero_field, stored_start)
    adjoint_state = (zero_field, jnp.zeros((slabs, width, width), jnp.float32))
    total_steps = levels + members - 1
    forward_state = lax.fori_loop(0, total_steps, forward_step, forward_state)
    stored_final = forward_state[1]
    adjoint_state = lax.fori_loop(
        0,
        total_steps,
        lambda moment, state: adjoint_step(moment, state, stored_final),
        adjoint_state,
    )
    return lax.psum_scatter(adjoint_state[1], "angle", scatter_dimension=1, tiled=True)


def solution(mesh):
    in_specs = (
        P(("blocks", "depth"), None, None),
        P(("blocks", "angle"), None, None),
        P(("blocks", "angle"), None),
        P(),
    )
    out_specs = P(("blocks", "depth"), "angle", None)
    return jax.shard_map(body, mesh=mesh, in_specs=in_specs, out_specs=out_specs, check_vma=False)
```

profile of v0, /device:TPU:0, one launch (start us, length us, event | category | flops | bytes accessed | tf_op | source)
XLA Modules:
  0.0 464.9 jit_solution(11775563196352999405)
XLA Ops:
  8.6 3.6 multiply_sine_fusion
  14.7 158.8 %while.49 = (s32[]{:T(128)}, f32[2,256,256]{2,1,0:T(8,128)S(1)}, f32[2,2,2,256,256]{4,3,2,1,0:T(8,128)}, s32[]{:T(128)}, s32[2,2]{1,0:T(2,128)S(1)}, /*index=5*/...) while((s32[]{:T(128)}, f32[2,256,256]{2,1,0:T(8,128)S(1)}, ...), condition=%wide.region_3.4_spmd.clone.clone.clone, body=%wide.region_0.3_spmd.clone.clone.clone.sunk | while | flops 6449201664 | bytes 42210792 | solution.py:166
  20.1 23.8 %conditional.12 = (f32[2,256,256]{2,1,0:T(8,128)}, f32[2,2,2,256,256]{4,3,2,1,0:T(8,128)}) conditional(s32[]{:T(128)} %convert_element_type.278, f32[2,2,2,256,256]{4,3,2,1,0:T(8,128)} %get-tuple-element.1735, (pred[]{:T(512)}, f32[2,256,256]{2,1,0:T(8,128)S(1)}, f32[2,256,256]{2,1,0:T(8,128)S(1)}, f32[512,512]{1,0:T(8,128)S(1)}, ...), branch_computations={%region_1.1_spmd, %region_2.2_spmd.clone} | conditional | flops 6445989888 | bytes 37748804 | solution.py:112
  40.9 2.1 fusion.37
  52.0 23.8 %conditional.12 = (f32[2,256,256]{2,1,0:T(8,128)}, f32[2,2,2,256,256]{4,3,2,1,0:T(8,128)}) conditional(s32[]{:T(128)} %convert_element_type.278, f32[2,2,2,256,256]{4,3,2,1,0:T(8,128)} %get-tuple-element.1735, (pred[]{:T(512)}, f32[2,256,256]{2,1,0:T(8,128)S(1)}, f32[2,256,256]{2,1,0:T(8,128)S(1)}, f32[512,512]{1,0:T(8,128)S(1)}, ...), branch_computations={%region_1.1_spmd, %region_2.2_spmd.clone} | conditional | flops 6445989888 | bytes 37748804 | solution.py:112
  63.0 1.9 fusion.140
  72.9 2.1 fusion.37
  75.8 2.3 collective-permute-start
  85.9 29.6 %collective-permute-start = (f32[2,256,256]{2,1,0:T(8,128)}, f32[2,256,256]{2,1,0:T(8,128)S(1)}, u32[]{:S(2)}, u32[]{:S(2)}) collective-permute-start(f32[2,256,256]{2,1,0:T(8,128)} %get-tuple-element.1687), channel_id=1, source_target_pairs={{0,4},{4,8},{8,12},{1,5},{5,9},{9,13},{2,6},{6,10},{10,14},{3,7},{... | collective-permute-start | bytes 1572872 | tf_op jit(solution)/shard_map/while/body/eval_jaxpr/ppermute | solution.py:15
  123.1 9.0 %collective-permute-start = (f32[2,256,256]{2,1,0:T(8,128)}, f32[2,256,256]{2,1,0:T(8,128)S(1)}, u32[]{:S(2)}, u32[]{:S(2)}) collective-permute-start(f32[2,256,256]{2,1,0:T(8,128)} %get-tuple-element.1687), channel_id=1, source_target_pairs={{0,4},{4,8},{8,12},{1,5},{5,9},{9,13},{2,6},{6,10},{10,14},{3,7},{... | collective-permute-start | bytes 1572872 | tf_op jit(solution)/shard_map/while/body/eval_jaxpr/ppermute | solution.py:15
  139.8 31.9 %collective-permute-start = (f32[2,256,256]{2,1,0:T(8,128)}, f32[2,256,256]{2,1,0:T(8,128)S(1)}, u32[]{:S(2)}, u32[]{:S(2)}) collective-permute-start(f32[2,256,256]{2,1,0:T(8,128)} %get-tuple-element.1687), channel_id=1, source_target_pairs={{0,4},{4,8},{8,12},{1,5},{5,9},{9,13},{2,6},{6,10},{10,14},{3,7},{... | collective-permute-start | bytes 1572872 | tf_op jit(solution)/shard_map/while/body/eval_jaxpr/ppermute | solution.py:15
  175.2 258.9 %while.50 = (s32[]{:T(128)}, f32[2,256,256]{2,1,0:T(8,128)}, f32[2,256,256]{2,1,0:T(8,128)}, s32[]{:T(128)}, s32[]{:T(128)}, /*index=5*/f32[2,2,2,256,256]{4,3,2...) while((s32[]{:T(128)}, f32[2,256,256]{2,1,0:T(8,128)}, ...), condition=%wide.region_9.10_spmd.clone.clone.clone, body=%wide.region_4.9_spmd.clone.clone.clone.sunk | while | flops 12893028352 | bytes 87034760 | solution.py:168
  203.1 9.3 %collective-permute-done.1 = f32[2,256,256]{2,1,0:T(8,128)S(1)} collective-permute-done((f32[2,256,256]{2,1,0:T(8,128)}, f32[2,256,256]{2,1,0:T(8,128)S(1)}, u32[]{:S(2)}, u32[]{:S(2)}) %collective-permute-start.1) | collective-permute-done | bytes 524320 | tf_op jit(solution)/shard_map/while/body/eval_jaxpr/ppermute | solution.py:15
  218.2 19.2 %collective-permute-done.1 = f32[2,256,256]{2,1,0:T(8,128)S(1)} collective-permute-done((f32[2,256,256]{2,1,0:T(8,128)}, f32[2,256,256]{2,1,0:T(8,128)S(1)}, u32[]{:S(2)}, u32[]{:S(2)}) %collective-permute-start.1) | collective-permute-done | bytes 524320 | tf_op jit(solution)/shard_map/while/body/eval_jaxpr/ppermute | solution.py:15
  243.3 101.7 %collective-permute-done.1 = f32[2,256,256]{2,1,0:T(8,128)S(1)} collective-permute-done((f32[2,256,256]{2,1,0:T(8,128)}, f32[2,256,256]{2,1,0:T(8,128)S(1)}, u32[]{:S(2)}, u32[]{:S(2)}) %collective-permute-start.1) | collective-permute-done | bytes 524320 | tf_op jit(solution)/shard_map/while/body/eval_jaxpr/ppermute | solution.py:15
  348.6 28.3 %conditional.13 = (f32[2,256,256]{2,1,0:T(8,128)}, f32[2,256,256]{2,1,0:T(8,128)}) conditional(s32[]{:T(128)} %convert_element_type.282, f32[2,256,256]{2,1,0:T(8,128)} %get-tuple-element.1782, (s32[]{:T(128)}, s32[]{:T(128)}, f32[2,2,2,256,256]{4,3,2,1,0:T(8,128)}, f32[2,256,256]{2,1,0:T(8,128)}, f32[512,512]{1,0:T(8,128)S(1)}, ...), branch_computations={%region_5.5_spmd, %region_6.8_spmd.clone} | conditional | flops 12890669056 | bytes 81527240 | solution.py:155
  348.7 2.4 constant_dynamic-slice_fusion.1
  372.2 1.9 fusion.150
  378.3 19.0 %collective-permute-done.1 = f32[2,256,256]{2,1,0:T(8,128)S(1)} collective-permute-done((f32[2,256,256]{2,1,0:T(8,128)}, f32[2,256,256]{2,1,0:T(8,128)S(1)}, u32[]{:S(2)}, u32[]{:S(2)}) %collective-permute-start.1) | collective-permute-done | bytes 524320 | tf_op jit(solution)/shard_map/while/body/eval_jaxpr/ppermute | solution.py:15
  401.0 28.3 %conditional.13 = (f32[2,256,256]{2,1,0:T(8,128)}, f32[2,256,256]{2,1,0:T(8,128)}) conditional(s32[]{:T(128)} %convert_element_type.282, f32[2,256,256]{2,1,0:T(8,128)} %get-tuple-element.1782, (s32[]{:T(128)}, s32[]{:T(128)}, f32[2,2,2,256,256]{4,3,2,1,0:T(8,128)}, f32[2,256,256]{2,1,0:T(8,128)}, f32[512,512]{1,0:T(8,128)S(1)}, ...), branch_computations={%region_5.5_spmd, %region_6.8_spmd.clone} | conditional | flops 12890669056 | bytes 81527240 | solution.py:155
  401.0 2.4 constant_dynamic-slice_fusion.1
  424.5 1.9 fusion.150
  430.6 2.7 collective-permute-done.1
  434.1 23.6 %reduce-scatter.2.cloned.1.call-done = f32[2,64,256]{2,1,0:T(8,128)} async-done(((f32[2,256,256]{2,1,0:T(8,128)}), f32[2,64,256]{2,1,0:T(8,128)}) %reduce-scatter.2.cloned.1.call-update) | async-done | bytes 131088 | tf_op jit(solution)/shard_map/reduce_scatter | solution.py:174
  (213 shorter events, 168.1 us)
Async XLA Ops:
  6.5 451.2 %reduce-scatter.2.cloned.1.call-start = ((), (), s32[]{:S(2)}) async-start(), calls=%async_computation.1 | async-start | bytes 655360 | tf_op jit(solution)/shard_map/reduce_scatter | solution.py:174
  12.8 1.8 copy-start.8
  43.9 3.0 collective-permute-start
  75.8 4.0 collective-permute-start
  85.9 31.3 %collective-permute-start = (f32[2,256,256]{2,1,0:T(8,128)}, f32[2,256,256]{2,1,0:T(8,128)S(1)}, u32[]{:S(2)}, u32[]{:S(2)}) collective-permute-start(f32[2,256,256]{2,1,0:T(8,128)} %get-tuple-element.1687), channel_id=1, source_target_pairs={{0,4},{4,8},{8,12},{1,5},{5,9},{9,13},{2,6},{6,10},{10,14},{3,7},{... | collective-permute-start | bytes 1572872 | tf_op jit(solution)/shard_map/while/body/eval_jaxpr/ppermute | solution.py:15
  123.1 10.7 %collective-permute-start = (f32[2,256,256]{2,1,0:T(8,128)}, f32[2,256,256]{2,1,0:T(8,128)S(1)}, u32[]{:S(2)}, u32[]{:S(2)}) collective-permute-start(f32[2,256,256]{2,1,0:T(8,128)} %get-tuple-element.1687), channel_id=1, source_target_pairs={{0,4},{4,8},{8,12},{1,5},{5,9},{9,13},{2,6},{6,10},{10,14},{3,7},{... | collective-permute-start | bytes 1572872 | tf_op jit(solution)/shard_map/while/body/eval_jaxpr/ppermute | solution.py:15
  139.8 33.6 %collective-permute-start = (f32[2,256,256]{2,1,0:T(8,128)}, f32[2,256,256]{2,1,0:T(8,128)S(1)}, u32[]{:S(2)}, u32[]{:S(2)}) collective-permute-start(f32[2,256,256]{2,1,0:T(8,128)} %get-tuple-element.1687), channel_id=1, source_target_pairs={{0,4},{4,8},{8,12},{1,5},{5,9},{9,13},{2,6},{6,10},{10,14},{3,7},{... | collective-permute-start | bytes 1572872 | tf_op jit(solution)/shard_map/while/body/eval_jaxpr/ppermute | solution.py:15
  201.8 10.6 %collective-permute-start.1 = (f32[2,256,256]{2,1,0:T(8,128)}, f32[2,256,256]{2,1,0:T(8,128)S(1)}, u32[]{:S(2)}, u32[]{:S(2)}) collective-permute-start(f32[2,256,256]{2,1,0:T(8,128)} %get-tuple-element.1704), channel_id=1, source_target_pairs={{4,0},{8,4},{12,8},{5,1},{9,5},{13,9},{6,2},{10,6},{14,10},{7,3},{... | collective-permute-start | bytes 1572872 | tf_op jit(solution)/shard_map/while/body/eval_jaxpr/ppermute | solution.py:15
  212.4 0.8 copy-start.7
  216.9 20.5 %collective-permute-start.1 = (f32[2,256,256]{2,1,0:T(8,128)}, f32[2,256,256]{2,1,0:T(8,128)S(1)}, u32[]{:S(2)}, u32[]{:S(2)}) collective-permute-start(f32[2,256,256]{2,1,0:T(8,128)} %get-tuple-element.1704), channel_id=1, source_target_pairs={{4,0},{8,4},{12,8},{5,1},{9,5},{13,9},{6,2},{10,6},{14,10},{7,3},{... | collective-permute-start | bytes 1572872 | tf_op jit(solution)/shard_map/while/body/eval_jaxpr/ppermute | solution.py:15
  237.5 0.8 copy-start.7
  242.0 103.0 %collective-permute-start.1 = (f32[2,256,256]{2,1,0:T(8,128)}, f32[2,256,256]{2,1,0:T(8,128)S(1)}, u32[]{:S(2)}, u32[]{:S(2)}) collective-permute-start(f32[2,256,256]{2,1,0:T(8,128)} %get-tuple-element.1704), channel_id=1, source_target_pairs={{4,0},{8,4},{12,8},{5,1},{9,5},{13,9},{6,2},{10,6},{14,10},{7,3},{... | collective-permute-start | bytes 1572872 | tf_op jit(solution)/shard_map/while/body/eval_jaxpr/ppermute | solution.py:15
  345.0 0.8 copy-start.7
  348.7 2.5 copy-start.2
  364.8 2.4 copy-start.5
  367.3 3.9 copy-start.6
  377.0 20.3 %collective-permute-start.1 = (f32[2,256,256]{2,1,0:T(8,128)}, f32[2,256,256]{2,1,0:T(8,128)S(1)}, u32[]{:S(2)}, u32[]{:S(2)}) collective-permute-start(f32[2,256,256]{2,1,0:T(8,128)} %get-tuple-element.1704), channel_id=1, source_target_pairs={{4,0},{8,4},{12,8},{5,1},{9,5},{13,9},{6,2},{10,6},{14,10},{7,3},{... | collective-permute-start | bytes 1572872 | tf_op jit(solution)/shard_map/while/body/eval_jaxpr/ppermute | solution.py:15
  397.3 0.8 copy-start.7
  401.0 2.5 copy-start.2
  417.1 2.4 copy-start.5
  419.6 3.9 copy-start.6
  429.3 4.0 collective-permute-start.1
  433.3 0.8 copy-start.7
Sparse Core Ops, SparseCore 0:
  434.3 23.4 reduce-scatter.1
where the time goes:
time: 469 us; the launch traced here: 465 us
  waiting for transfers between devices  184 us (39%)
  starting transfers between devices  80.5 us (17%)
  other arithmetic  70.3 us (15%)
  matrix products  61.7 us (13%)
  local copies, waits for them, and re-layouts  29.3 us (6%)
  loops' own time  24.6 us (5%)
  between operations  14.5 us (3%)
    ppermute x10, waiting for transfers between devices, passed_along(): return lax.ppermute(shard, axis, pairs)  160 us
    ppermute x10, starting transfers between devices, passed_along(): return lax.ppermute(shard, axis, pairs)  80.5 us
    dot_general x16, matrix products, transform(): left = jnp.dot(big, field.reshape(2 * width, width), precision=highest)  29.8 us
    reduce_scatter x1, waiting for transfers between devices, body(): lax.psum_scatter(adjoint_state[1], 'angle', scatter_dimension=1, tiled=True)  23.6 us
    another operation x1, loops' own time, body(): lax.fori_loop(0, total_steps, lambda moment, state: adjoint_step(moment,...  23 us
    dot_general x16, matrix products, transform(): imag_part = jnp.dot(left, part_im, precision=highest)  16 us
    dot_general x16, matrix products, transform(): real_part = jnp.dot(left, part_re, precision=highest)  15.9 us
    another operation x28, other arithmetic, complex_mul(): jnp.stack([field[0] * mult_re - field[1] * mult_im, field[0] * mult_im +...  13.7 us
  transfers between devices with their start and end apart: 11, of which 11 were waited for; matrix products, arithmetic and copies ran while one was open for 0% of the time, Pallas kernels for 0%

commit v1 on v0

v1 whole, which is shorter than its diff:
```python
import functools
import math

import jax
import jax.numpy as jnp
import numpy as np
from jax import lax
from jax.experimental import pallas as pl
from jax.experimental.pallas import tpu as pltpu
from jax.sharding import PartitionSpec as P

screen_scale = 0.25
F32 = jnp.float32
BF16 = jnp.bfloat16


def tables(width):
    index = np.arange(width)
    turn = 2.0 * np.pi / width * (index[:, None] * index[None, :] % width)
    hartley = ((np.cos(turn) + np.sin(turn)) / math.sqrt(width)).astype(np.float32)
    high = hartley.astype(BF16)
    low = (hartley - high.astype(np.float32)).astype(BF16)
    freq = (index + width // 2) % width - width // 2
    square = (freq[:, None] ** 2 + freq[None, :] ** 2).astype(np.float64)
    phi = 13.0 / width * (np.sqrt(0.64 * width * width - square) - 0.8 * width)
    wave = np.stack([np.cos(phi), np.sin(phi)]).astype(np.float32)
    return (
        np.concatenate([high, high, low], 1),
        np.concatenate([high, high, low], 0),
        wave,
        square.astype(np.float32),
    )


def halves(value):
    high = value.astype(BF16)
    return high, (value - high.astype(F32)).astype(BF16)


def sincos_small(angle):
    sq = angle * angle
    cosine = 1.0 + sq * (
        -0.5 + sq * (1 / 24 + sq * (-1 / 720 + sq * (1 / 40320 - sq * (1 / 3628800))))
    )
    sine = angle * (
        1.0 + sq * (-1 / 6 + sq * (1 / 120 + sq * (-1 / 5040 + sq * (1 / 362880))))
    )
    return cosine, sine


def sincos_steps(steps, width):
    steps = steps & (width - 1)
    quarter = width // 4
    turns = (steps + quarter // 2) // quarter
    rest = (steps - turns * quarter).astype(F32) * (2.0 * math.pi / width)
    cosine, sine = sincos_small(rest)
    turns = turns & 3
    swap = (turns & 1) == 1
    first = jnp.where(swap, sine, cosine)
    second = jnp.where(swap, cosine, sine)
    first = jnp.where((turns == 1) | (turns == 2), -first, first)
    second = jnp.where(turns >= 2, -second, second)
    return first, second


def columns_mixed(pair, right_ref):
    high, low = halves(pair)
    return jnp.dot(
        jnp.concatenate([high, low, high], 1), right_ref[...], preferred_element_type=F32
    )


def rows_mixed(value, left_ref):
    high, low = halves(value)
    return jnp.dot(
        left_ref[...], jnp.concatenate([high, low, high], 0), preferred_element_type=F32
    )


def filtered(real, imag, mult_re, mult_im, left_ref, right_ref):
    width = real.shape[0]
    mixed = columns_mixed(jnp.concatenate([real, imag], 0), right_ref)
    real = rows_mixed(mixed[:width], left_ref)
    imag = rows_mixed(mixed[width:], left_ref)
    if mult_im is None:
        real, imag = real * mult_re, imag * mult_re
    else:
        real, imag = real * mult_re - imag * mult_im, real * mult_im + imag * mult_re
    real = rows_mixed(real, left_ref)
    imag = rows_mixed(imag, left_ref)
    mixed = columns_mixed(jnp.concatenate([real, imag], 0), right_ref)
    return mixed[:width], mixed[width:]


def kernel(
    pair_ref, cutoff_ref, index_ref, target_ref, left_ref, right_ref, wave_ref, square_ref,
    term_ref, field_ref, screen_ref, adjoint_ref,
):
    slices, width = index_ref.shape[0], index_ref.shape[1]
    kx, ky = pair_ref[0], pair_ref[1]
    whole = jnp.full((8, 128), kx * kx + ky * ky, jnp.int32).astype(F32)
    phi = 13.0 / width * (jnp.sqrt(0.64 * width * width - whole) - 0.8 * width)
    lead_re, lead_im = jnp.cos(phi)[:1, :1], jnp.sin(phi)[:1, :1]
    row_re, row_im = sincos_steps(
        kx * lax.broadcasted_iota(jnp.int32, (width, 1), 0), width
    )
    col_re, col_im = sincos_steps(
        ky * lax.broadcasted_iota(jnp.int32, (1, width), 1), width
    )
    row_re, row_im = row_re * lead_re - row_im * lead_im, row_re * lead_im + row_im * lead_re

    def screened(level, real, imag):
        screen_re, screen_im = sincos_small(screen_scale * index_ref[level])
        screen_ref[level, 0] = screen_re
        screen_ref[level, 1] = screen_im
        field_ref[level, 0] = real * screen_re - imag * screen_im
        field_ref[level, 1] = real * screen_im + imag * screen_re

    screened(0, row_re * col_re - row_im * col_im, row_re * col_im + row_im * col_re)

    def forward(level, carry):
        real, imag = filtered(
            field_ref[level - 1, 0], field_ref[level - 1, 1],
            wave_ref[0], wave_ref[1], left_ref, right_ref,
        )
        screened(level, real, imag)
        return carry

    lax.fori_loop(1, slices, forward, 0)
    cutoff = cutoff_ref[0]
    limit = (cutoff * cutoff).astype(F32)
    adjoint_ref[0] = field_ref[slices - 1, 0]
    adjoint_ref[1] = field_ref[slices - 1, 1]

    def through_pupil(turn, carry):
        pupil = (square_ref[...] <= limit).astype(F32)
        real, imag = filtered(
            adjoint_ref[0], adjoint_ref[1], pupil, None, left_ref, right_ref
        )
        misfit = 2.0 * (real * real + imag * imag - target_ref[...])
        misfit = jnp.where(turn == 0, misfit, 1.0)
        adjoint_ref[0] = misfit * real
        adjoint_ref[1] = misfit * imag
        return carry

    lax.fori_loop(0, 2, through_pupil, 0)

    def with_term(level):
        real, imag = adjoint_ref[0], adjoint_ref[1]
        term_ref[level] = screen_scale * (
            field_ref[level, 0] * imag - field_ref[level, 1] * real
        )
        return real, imag

    def backward(step, carry):
        level = slices - 1 - step
        real, imag = with_term(level)
        screen_re, screen_im = screen_ref[level, 0], screen_ref[level, 1]
        real, imag = real * screen_re + imag * screen_im, imag * screen_re - real * screen_im
        real, imag = filtered(
            real, imag, wave_ref[0], -wave_ref[1], left_ref, right_ref
        )
        adjoint_ref[0] = real
        adjoint_ref[1] = imag
        return carry

    lax.fori_loop(0, slices - 1, backward, 0)
    with_term(0)


def body(index_change, measured, angle_index, cutoff):
    width = index_change.shape[1]
    members = measured.shape[0]
    place = lax.axis_index("depth")
    whole = lax.all_gather(index_change, "depth", axis=0, tiled=True)
    slices = whole.shape[0]
    member = place % members
    target = lax.dynamic_index_in_dim(measured, member, 0, keepdims=False)
    pair = lax.dynamic_index_in_dim(angle_index, member, 0, keepdims=False)
    left, right, wave, square = tables(width)
    smem = pl.BlockSpec(memory_space=pltpu.SMEM)
    vmem = pl.BlockSpec(memory_space=pltpu.VMEM)
    terms = pl.pallas_call(
        kernel,
        out_shape=jax.ShapeDtypeStruct((slices, width, width), F32),
        in_specs=[smem] * 2 + [vmem] * 6,
        out_specs=vmem,
        scratch_shapes=[
            pltpu.VMEM((slices, 2, width, width), F32),
            pltpu.VMEM((slices, 2, width, width), F32),
            pltpu.VMEM((2, width, width), F32),
        ],
        compiler_params=pltpu.CompilerParams(vmem_limit_bytes=56 * 2**20),
    )(pair, cutoff, whole, target, left, right, wave, square)
    terms = jnp.where(place < members, terms, 0.0)
    terms = lax.psum_scatter(terms, "depth", scatter_dimension=0, tiled=True)
    return lax.psum_scatter(terms, "angle", scatter_dimension=1, tiled=True)


def solution(mesh):
    in_specs = (
        P(("blocks", "depth"), None, None),
        P(("blocks", "angle"), None, None),
        P(("blocks", "angle"), None),
        P(),
    )
    out_specs = P(("blocks", "depth"), "angle", None)
    return jax.shard_map(body, mesh=mesh, in_specs=in_specs, out_specs=out_specs, check_vma=False)
```

time: 469 us -> 130 us (0.28)
  waiting for transfers between devices: 184 us -> 80.7 us
  starting transfers between devices: 80.5 us -> 0.08 us
  other arithmetic: 70.3 us -> 3.09 us
  matrix products: 61.7 us -> 0 us
  Pallas kernels: 0 us -> 30.8 us
  local copies, waits for them, and re-layouts: 29.3 us -> 1.92 us
  loops' own time: 24.6 us -> 0 us
    ppermute x10 -> x0, waiting for transfers between devices: 160 us -> none  [passed_along(): return lax.ppermute(shard, axis, pairs)]
    ppermute x10 -> x0, starting transfers between devices: 80.5 us -> none  [passed_along(): return lax.ppermute(shard, axis, pairs)]
    dot_general x48 -> x0, matrix products: 61.7 us -> none  [the longest x16 29.8 us: transform(): left = jnp.dot(big, field.reshape(2 * width, width), precision=highest)]
    reduce_scatter x1 -> x2, waiting for transfers between devices: 23.6 us -> 55.6 us  [the longest x1 31.6 us: body(): terms = lax.psum_scatter(terms, 'depth', scatter_dimension=0, tiled=True)]
    pallas_call x0 -> x1, Pallas kernels: none -> 30.8 us  [body(): pl.pallas_call(kernel, out_shape=jax.ShapeDtypeStruct((slices, width, wid...]
    another operation x14 -> x0, loops' own time: 24.6 us -> none  [the longest x1 23 us: body(): lax.fori_loop(0, total_steps, lambda moment, state: adjoint_step(moment,...]
    all_gather x0 -> x1, waiting for transfers between devices: none -> 24.4 us  [body(): whole = lax.all_gather(index_change, 'depth', axis=0, tiled=True)]
    another operation x41 -> x0, other arithmetic: 17.5 us -> none  [the longest x28 13.7 us: complex_mul(): jnp.stack([field[0] * mult_re - field[1] * mult_im, field[0] * mult_im +...]
  transfers between devices with their start and end apart: 11 -> 3, of which waited for: 11 -> 3; matrix products, arithmetic and copies ran while one was open for 0% -> 1% of each run, Pallas kernels for 0% -> 0%
where the time goes in v1:
time: 130 us
  waiting for transfers between devices  80.7 us (62%)
  Pallas kernels  30.8 us (24%)
  between operations  13.8 us (11%)
  other arithmetic  3.09 us (2%)
  local copies, waits for them, and re-layouts  1.92 us (1%)
    reduce_scatter x1, waiting for transfers between devices, body(): terms = lax.psum_scatter(terms, 'depth', scatter_dimension=0, tiled=True)  31.6 us
    pallas_call x1, Pallas kernels, body(): pl.pallas_call(kernel, out_shape=jax.ShapeDtypeStruct((slices, width, wid...  30.8 us
    all_gather x1, waiting for transfers between devices, body(): whole = lax.all_gather(index_change, 'depth', axis=0, tiled=True)  24.4 us
    reduce_scatter x1, waiting for transfers between devices, body(): return lax.psum_scatter(terms, 'angle', scatter_dimension=1, tiled=True)  24 us
    select_n x1, other arithmetic, body(): terms = jnp.where(place < members, terms, 0.0)  3.09 us
  transfers between devices with their start and end apart: 3, of which 3 were waited for; matrix products, arithmetic and copies ran while one was open for 1% of the time, Pallas kernels for 0%

profile of v1, /device:TPU:0, one launch (start us, length us, event | category | flops | bytes accessed | tf_op | source)
XLA Modules:
  0.0 130.3 jit_solution(136823506492172994)
XLA Ops:
  6.5 0.0 copy-start
  6.5 0.0 all-gather.2.cloned.1.call-start
  6.5 0.7 all-gather.2.cloned.1.call-update
  7.3 0.0 reduce-scatter.3.cloned.1.call-start
  8.0 1.2 dynamic-slice_bitcast_fusion.1.pair_ref
  9.2 0.0 copy-done
  9.2 0.7 dynamic-slice_bitcast_fusion.target_ref
  9.9 24.4 %all-gather.2.cloned.1.call-done.index_ref = f32[8,256,256]{2,1,0:T(8,128)} async-done(((f32[2,256,256]{2,1,0:T(8,128)}), f32[8,256,256]{2,1,0:T(8,128)}) %all-gather.2.cloned.1.call-update) | async-done | bytes 2097168 | tf_op jit(solution)/shard_map/all_gather | solution.py:175
  34.2 30.8 %shard_map.82 = f32[8,256,256]{2,1,0:T(8,128)} custom-call(s32[2]{0:T(128)} %dynamic-slice_bitcast_fusion.1.pair_ref, s32[1]{0:T(128)S(6)} %copy.9.cutoff_ref, f32[8,256,256]{2,1,0:T(8,128)} %all-gather.2.cloned.1.call-done.index_ref, f32[256,256]{1,0:T(8,128)} %dynamic-slice_bitcast_fusion.target_ref, bf16[256,768]{1,0:T(8,128)(2,1)} %constant.36.clone.left_ref, ...), custom_call_target="tpu_custom_call" | custom-call | tf_op jit(solution)/shard_map/pallas_call | solution.py:183
  65.0 3.1 %broadcast_select_fusion = f32[8,256,256]{2,1,0:T(8,128)} fusion(f32[8,256,256]{2,1,0:T(8,128)} %shard_map.82, pred[]{:T(512)S(6)} %lt.15), kind=kLoop, calls=%fused_computation | loop fusion | flops 524288 | bytes 4194305 | tf_op jit(solution)/shard_map/jit(_where)/select_n | solution.py:195
  68.1 0.0 reduce-scatter.3.cloned.1.call-update
  68.1 0.0 reduce-scatter.5.cloned.1.call-start
  68.2 31.6 %reduce-scatter.3.cloned.1.call-done = f32[2,256,256]{2,1,0:T(8,128)} async-done(((f32[8,256,256]{2,1,0:T(8,128)}), f32[2,256,256]{2,1,0:T(8,128)}) %reduce-scatter.3.cloned.1.call-update) | async-done | bytes 524304 | tf_op jit(solution)/shard_map/reduce_scatter | solution.py:196
  99.7 0.0 reduce-scatter.5.cloned.1.call-update
  99.8 24.0 %reduce-scatter.5.cloned.1.call-done = f32[2,64,256]{2,1,0:T(8,128)} async-done(((f32[2,256,256]{2,1,0:T(8,128)}), f32[2,64,256]{2,1,0:T(8,128)}) %reduce-scatter.5.cloned.1.call-update) | async-done | bytes 131088 | tf_op jit(solution)/shard_map/reduce_scatter | solution.py:197
Async XLA Ops:
  6.5 2.6 %copy-start = (f32[2,256,256]{2,1,0:T(8,128)S(1)}, f32[2,256,256]{2,1,0:T(8,128)}, u32[]{:S(2)}) copy-start(f32[2,256,256]{2,1,0:T(8,128)} %param.9) | copy-start | bytes 1572868
  6.5 27.7 %all-gather.2.cloned.1.call-start = ((), (), s32[]{:S(2)}) async-start(), calls=%async_computation.2 | async-start | bytes 2621440 | tf_op jit(solution)/shard_map/all_gather | solution.py:175
  7.3 92.5 %reduce-scatter.3.cloned.1.call-start = ((), (), s32[]{:S(2)}) async-start(), calls=%async_computation.3 | async-start | bytes 2621440 | tf_op jit(solution)/shard_map/reduce_scatter | solution.py:196
  68.1 55.7 %reduce-scatter.5.cloned.1.call-start = ((), (), s32[]{:S(2)}) async-start(), calls=%async_computation.4 | async-start | bytes 655360 | tf_op jit(solution)/shard_map/reduce_scatter | solution.py:197
Sparse Core Ops, SparseCore 0:
  8.9 25.2 all-gather.1
  68.3 31.4 reduce-scatter.2
  102.1 21.6 reduce-scatter.4

commit v2 on v1

v2 whole, which is shorter than its diff:
```python
import math

import jax
import jax.numpy as jnp
import numpy as np
from jax import lax
from jax.experimental import pallas as pl
from jax.experimental.pallas import tpu as pltpu
from jax.sharding import PartitionSpec as P

screen_scale = 0.25
F32 = jnp.float32
BF16 = jnp.bfloat16


def tables(width):
    index = np.arange(width)
    turn = 2.0 * np.pi / width * (index[:, None] * index[None, :] % width)
    hartley = ((np.cos(turn) + np.sin(turn)) / math.sqrt(width)).astype(np.float32)
    high = hartley.astype(BF16)
    low = (hartley - high.astype(np.float32)).astype(BF16)
    freq = (index + width // 2) % width - width // 2
    square = (freq[:, None] ** 2 + freq[None, :] ** 2).astype(np.float64)
    phi = 13.0 / width * (np.sqrt(0.64 * width * width - square) - 0.8 * width)
    wave = np.stack([np.cos(phi), np.sin(phi)]).astype(np.float32)
    return (
        np.concatenate([high, high, low], 1),
        np.concatenate([high, high, low], 0),
        wave,
        square.astype(np.float32),
    )


def halves(value):
    high = value.astype(BF16)
    return high, (value - high.astype(F32)).astype(BF16)


def sincos_small(angle):
    sq = angle * angle
    cosine = 1.0 + sq * (
        -0.5 + sq * (1 / 24 + sq * (-1 / 720 + sq * (1 / 40320 - sq * (1 / 3628800))))
    )
    sine = angle * (
        1.0 + sq * (-1 / 6 + sq * (1 / 120 + sq * (-1 / 5040 + sq * (1 / 362880))))
    )
    return cosine, sine


def sincos_steps(steps, width):
    steps = steps & (width - 1)
    quarter = width // 4
    turns = (steps + quarter // 2) // quarter
    rest = (steps - turns * quarter).astype(F32) * (2.0 * math.pi / width)
    cosine, sine = sincos_small(rest)
    turns = turns & 3
    swap = (turns & 1) == 1
    first = jnp.where(swap, sine, cosine)
    second = jnp.where(swap, cosine, sine)
    first = jnp.where((turns == 1) | (turns == 2), -first, first)
    second = jnp.where(turns >= 2, -second, second)
    return first, second


def columns_mixed(pair, right_ref):
    high, low = halves(pair)
    return jnp.dot(
        jnp.concatenate([high, low, high], 1), right_ref[...], preferred_element_type=F32
    )


def rows_mixed(value, left_ref):
    high, low = halves(value)
    return jnp.dot(
        left_ref[...], jnp.concatenate([high, low, high], 0), preferred_element_type=F32
    )


def filtered(real, imag, mult_re, mult_im, left_ref, right_ref):
    width = real.shape[0]
    mixed = columns_mixed(jnp.concatenate([real, imag], 0), right_ref)
    real = rows_mixed(mixed[:width], left_ref)
    imag = rows_mixed(mixed[width:], left_ref)
    if mult_im is None:
        real, imag = real * mult_re, imag * mult_re
    else:
        real, imag = real * mult_re - imag * mult_im, real * mult_im + imag * mult_re
    real = rows_mixed(real, left_ref)
    imag = rows_mixed(imag, left_ref)
    mixed = columns_mixed(jnp.concatenate([real, imag], 0), right_ref)
    return mixed[:width], mixed[width:]


MESH = pl.DeviceIdType.MESH


def kernel(
    pair_ref, cutoff_ref, index_ref, target_ref, left_ref, right_ref, wave_ref, square_ref,
    out_ref,
    gathered_ref, field_ref, adjoint_ref, term_ref, inbox_ref, total_ref, part_ref,
    own_send, relay_send, gather_recv, term_send, term_recv, sum_send, sum_recv,
    part_send, part_recv, turn_sem,
):
    slabs, width = index_ref.shape[0], index_ref.shape[1]
    slices = gathered_ref.shape[0]
    members = target_ref.shape[0]
    levels, angles = lax.axis_size("depth"), lax.axis_size("angle")
    rows = width // angles
    place, spoke = lax.axis_index("depth"), lax.axis_index("angle")
    worker = place < members

    barrier = pltpu.get_barrier_semaphore()
    for step in range(1, levels):
        pl.semaphore_signal(
            barrier, device_id={"depth": lax.rem(place + step, levels)}, device_id_type=MESH
        )
    for step in range(1, angles):
        pl.semaphore_signal(
            barrier, device_id={"angle": lax.rem(spoke + step, angles)}, device_id_type=MESH
        )
    pl.semaphore_wait(barrier, levels + angles - 2)

    def remote(source, target, send, recv, device):
        return pltpu.make_async_remote_copy(
            src_ref=source, dst_ref=target, send_sem=send, recv_sem=recv,
            device_id=device, device_id_type=MESH,
        )

    def own_copy(slab, step):
        level = place * slabs + slab
        return remote(
            index_ref.at[slab], gathered_ref.at[level], own_send.at[slab, step],
            gather_recv.at[level], {"depth": lax.rem(place + step, members)},
        )

    def relay_copy(level, step):
        return remote(
            gathered_ref.at[level], gathered_ref.at[level], relay_send.at[level, step],
            gather_recv.at[level], {"depth": lax.rem(place + step, members)},
        )

    def term_copy(level):
        entry = (level // slabs) % members
        slot = lax.rem(place - entry + members, members)
        return remote(
            term_ref.at[level], inbox_ref.at[level, slot], term_send.at[level],
            term_recv.at[level, slot], {"depth": entry},
        )

    def sum_copy(level):
        return remote(
            term_ref.at[level], total_ref.at[level % slabs], sum_send.at[level],
            sum_recv.at[level % slabs], {"depth": level // slabs},
        )

    def part_copy(slab, step):
        goal = lax.rem(spoke + step, angles)
        return remote(
            total_ref.at[slab, pl.ds(pl.multiple_of(goal * rows, rows), rows)],
            part_ref.at[slab, step], part_send.at[slab, step], part_recv.at[slab, step],
            {"angle": goal},
        )

    def start_parts(slab):
        for step in range(1, angles):
            part_copy(slab, step).start()

    @pl.when(jnp.logical_not(worker))
    def _():
        @pl.when(place > members)
        def _():
            pl.semaphore_wait(turn_sem, 1)

        for slab in range(slabs):
            copy = own_copy(slab, 0)
            copy.start()
            copy.wait_send()

        @pl.when(place < levels - 1)
        def _():
            pl.semaphore_signal(turn_sem, device_id={"depth": lax.rem(place + 1, levels)}, device_id_type=MESH)

        for slab in reversed(range(slabs)):
            sum_copy(place * slabs + slab).wait_recv()
            start_parts(slab)

    def work():
        kx, ky = pair_ref[place, 0], pair_ref[place, 1]
        whole = jnp.full((8, 128), kx * kx + ky * ky, jnp.int32).astype(F32)
        phi = 13.0 / width * (jnp.sqrt(0.64 * width * width - whole) - 0.8 * width)
        lead_re, lead_im = jnp.cos(phi)[:1, :1], jnp.sin(phi)[:1, :1]
        row_re, row_im = sincos_steps(
            kx * lax.broadcasted_iota(jnp.int32, (width, 1), 0), width
        )
        col_re, col_im = sincos_steps(
            ky * lax.broadcasted_iota(jnp.int32, (1, width), 1), width
        )
        row_re, row_im = row_re * lead_re - row_im * lead_im, row_re * lead_im + row_im * lead_re

        def relay(level):
            owner = level // slabs

            @pl.when((owner >= members) & (owner % members == place) & (level < slices))
            def _():
                relay_copy(level, 0).wait_recv()
                for step in range(1, members):
                    relay_copy(level, step).start()

        def ready(level):
            owner = level // slabs

            @pl.when((owner != place) & ((owner < members) | (owner % members != place)))
            def _():
                relay_copy(level, 0).wait_recv()

        def screened(level, real, imag):
            screen_re, screen_im = sincos_small(screen_scale * gathered_ref[level])
            field_ref[level, 0] = real * screen_re - imag * screen_im
            field_ref[level, 1] = real * screen_im + imag * screen_re

        relay(0)
        relay(1)
        ready(0)
        screened(0, row_re * col_re - row_im * col_im, row_re * col_im + row_im * col_re)

        def forward(level, carry):
            real, imag = filtered(
                field_ref[level - 1, 0], field_ref[level - 1, 1],
                wave_ref[0], wave_ref[1], left_ref, right_ref,
            )
            relay(level + 1)
            ready(level)
            screened(level, real, imag)
            return carry

        lax.fori_loop(1, slices, forward, 0)
        cutoff = cutoff_ref[0]
        limit = (cutoff * cutoff).astype(F32)
        adjoint_ref[0] = field_ref[slices - 1, 0]
        adjoint_ref[1] = field_ref[slices - 1, 1]

        def through_pupil(turn, carry):
            pupil = (square_ref[...] <= limit).astype(F32)
            real, imag = filtered(
                adjoint_ref[0], adjoint_ref[1], pupil, None, left_ref, right_ref
            )
            misfit = 2.0 * (real * real + imag * imag - target_ref[place])
            misfit = jnp.where(turn == 0, misfit, 1.0)
            adjoint_ref[0] = misfit * real
            adjoint_ref[1] = misfit * imag
            return carry

        lax.fori_loop(0, 2, through_pupil, 0)

        def with_term(level):
            real, imag = adjoint_ref[0], adjoint_ref[1]
            term_ref[level] = screen_scale * (
                field_ref[level, 0] * imag - field_ref[level, 1] * real
            )

            @pl.when((level // slabs) % members != place)
            def _():
                term_copy(level).start()

            return real, imag

        def pass_on(level):
            owner = level // slabs

            @pl.when(owner % members == place)
            def _():
                value = term_ref[level]
                for slot in range(1, members):
                    remote(
                        inbox_ref.at[level, slot], inbox_ref.at[level, slot],
                        term_send.at[level], term_recv.at[level, slot], {"depth": lax.rem(place + 1, levels)},
                    ).wait_recv()
                    value = value + inbox_ref[level, slot]

                @pl.when(owner == place)
                def _():
                    total_ref[level % slabs] = value
                    start_parts(level % slabs)

                @pl.when(owner != place)
                def _():
                    term_ref[level] = value
                    sum_copy(level).start()

        def backward(step, carry):
            level = slices - 1 - step
            real, imag = with_term(level)
            screen_re, screen_im = sincos_small(screen_scale * gathered_ref[level])
            real, imag = real * screen_re + imag * screen_im, imag * screen_re - real * screen_im
            real, imag = filtered(
                real, imag, wave_ref[0], -wave_ref[1], left_ref, right_ref
            )
            adjoint_ref[0] = real
            adjoint_ref[1] = imag
            pass_on(level)
            return carry

        lax.fori_loop(0, slices - 1, backward, 0)
        with_term(0)
        pass_on(0)

    @pl.when(worker)
    def _():
        for slab in range(slabs):
            for step in range(1, members):
                own_copy(slab, step).start()
        for slab in range(slabs):
            gathered_ref[place * slabs + slab] = index_ref[slab]
        work()

    for slab in reversed(range(slabs)):
        value = total_ref[slab, pl.ds(pl.multiple_of(spoke * rows, rows), rows)]
        for step in range(1, angles):
            part_copy(slab, step).wait_recv()
            value = value + part_ref[slab, step]
        out_ref[slab] = value

    for slab in range(slabs):
        for step in range(1, angles):
            part_copy(slab, step).wait_send()

    @pl.when(worker)
    def _():
        for slab in range(slabs):
            for step in range(1, members):
                own_copy(slab, step).wait_send()

        def finish(level, carry):
            owner = level // slabs
            entry = owner % members

            @pl.when((owner >= members) & (entry == place))
            def _():
                for step in range(1, members):
                    relay_copy(level, step).wait_send()
                sum_copy(level).wait_send()

            @pl.when(entry != place)
            def _():
                term_copy(level).wait_send()

            return carry

        lax.fori_loop(0, slices, finish, 0)


def body(index_change, measured, angle_index, cutoff):
    slabs, width = index_change.shape[0], index_change.shape[1]
    members = measured.shape[0]
    levels, angles = lax.axis_size("depth"), lax.axis_size("angle")
    slices = slabs * levels
    left, right, wave, square = tables(width)
    smem = pl.BlockSpec(memory_space=pltpu.SMEM)
    vmem = pl.BlockSpec(memory_space=pltpu.VMEM)
    sem = pltpu.SemaphoreType.DMA
    return pl.pallas_call(
        kernel,
        out_shape=jax.ShapeDtypeStruct((slabs, width // angles, width), F32),
        in_specs=[smem] * 2 + [vmem] * 6,
        out_specs=vmem,
        scratch_shapes=[
            pltpu.VMEM((slices, width, width), F32),
            pltpu.VMEM((slices, 2, width, width), F32),
            pltpu.VMEM((2, width, width), F32),
            pltpu.VMEM((slices, width, width), F32),
            pltpu.VMEM((slices, members, width, width), F32),
            pltpu.VMEM((slabs, width, width), F32),
            pltpu.VMEM((slabs, angles, width // angles, width), F32),
            sem((slabs, members)),
            sem((slices, members)),
            sem((slices,)),
            sem((slices,)),
            sem((slices, members)),
            sem((slices,)),
            sem((slabs,)),
            sem((slabs, angles)),
            sem((slabs, angles)),
            pltpu.SemaphoreType.REGULAR,
        ],
        compiler_params=pltpu.CompilerParams(
            collective_id=0, has_side_effects=True, vmem_limit_bytes=60 * 2**20
        ),
    )(angle_index, cutoff, index_change, measured, left, right, wave, square)


def solution(mesh):
    in_specs = (
        P(("blocks", "depth"), None, None),
        P(("blocks", "angle"), None, None),
        P(("blocks", "angle"), None),
        P(),
    )
    out_specs = P(("blocks", "depth"), "angle", None)
    return jax.shard_map(body, mesh=mesh, in_specs=in_specs, out_specs=out_specs, check_vma=False)
```

time: 130 us -> 54.2 us (0.42)
  waiting for transfers between devices: 80.7 us -> 0 us
  Pallas kernels: 30.8 us -> 51.8 us
  between operations: 13.8 us -> 0.66 us
  other arithmetic: 3.09 us -> 0 us
    reduce_scatter x2 -> x0, waiting for transfers between devices: 55.6 us -> none  [the longest x1 31.6 us: body(): terms = lax.psum_scatter(terms, 'depth', scatter_dimension=0, tiled=True)]
    all_gather x1 -> x0, waiting for transfers between devices: 24.4 us -> none  [body(): whole = lax.all_gather(index_change, 'depth', axis=0, tiled=True)]
    pallas_call x1, Pallas kernels: 30.8 us -> 51.8 us  [body(): pl.pallas_call(kernel, out_shape=jax.ShapeDtypeStruct((slabs, width // an...]
    select_n x1 -> x0, other arithmetic: 3.09 us -> none  [body(): terms = jnp.where(place < members, terms, 0.0)]
    squeeze x2 -> x0, local copies, waits for them, and re-layouts: 1.91 us -> none  [the longest x1 1.2 us: body(): pair = lax.dynamic_index_in_dim(angle_index, member, 0, keepdims=False)]
    unnamed x2 -> x1, local copies, waits for them, and re-layouts: 0.01 us -> 1.57 us
  transfers between devices with their start and end apart: 3 -> 0, of which waited for: 3 -> 0; matrix products, arithmetic and copies ran while one was open for 1% -> 0% of each run, Pallas kernels for 0% -> 0%
where the time goes in v2:
time: 54.2 us; the launch traced here: 54 us
  Pallas kernels  51.8 us (96%)
  local copies, waits for them, and re-layouts  1.57 us (3%)
  between operations  0.66 us (1%)
    pallas_call x1, Pallas kernels, body(): pl.pallas_call(kernel, out_shape=jax.ShapeDtypeStruct((slabs, width // an...  51.8 us
    unnamed x1, local copies, waits for them, and re-layouts  1.57 us

profile of v2, /device:TPU:0, one launch (start us, length us, event | category | flops | bytes accessed | tf_op | source)
XLA Modules:
  0.0 54.0 jit_solution(1258087945686412855)
XLA Ops:
  0.7 51.8 %shard_map.82 = f32[2,64,256]{2,1,0:T(8,128)} custom-call(s32[2,2]{1,0:T(2,128)} %pair_ref.1, s32[1]{0:T(128)S(6)} %copy.10.cutoff_ref, f32[2,256,256]{2,1,0:T(8,128)} %index_ref.1, f32[2,256,256]{2,1,0:T(8,128)} %target_ref.1, bf16[256,768]{1,0:T(8,128)(2,1)} %constant.8.clone.left_ref, bf16[768,256]{1,0:T(8,128)(2,1)} %constant.9.clone.right_ref, ...), custom_call_target="tpu_custom_call" | custom-call | tf_op jit(solution)/shard_map/pallas_call | solution.py:361
  52.5 1.6 %copy.11 = f32[2,64,256]{2,1,0:T(8,128)} copy(f32[2,64,256]{2,1,0:T(8,128)} %shard_map.82) | data formatting | bytes 262144

commit v3 on v2

--- a/solution.py
+++ b/solution.py
@@ -23,12 +23,7 @@
     square = (freq[:, None] ** 2 + freq[None, :] ** 2).astype(np.float64)
     phi = 13.0 / width * (np.sqrt(0.64 * width * width - square) - 0.8 * width)
     wave = np.stack([np.cos(phi), np.sin(phi)]).astype(np.float32)
-    return (
-        np.concatenate([high, high, low], 1),
-        np.concatenate([high, high, low], 0),
-        wave,
-        square.astype(np.float32),
-    )
+    return np.stack([high, low]), wave
 
 
 def halves(value):
@@ -62,32 +57,36 @@
     return first, second
 
 
-def columns_mixed(pair, right_ref):
+def columns_mixed(pair, mix_ref):
     high, low = halves(pair)
-    return jnp.dot(
-        jnp.concatenate([high, low, high], 1), right_ref[...], preferred_element_type=F32
+    return (
+        jnp.dot(high, mix_ref[0], preferred_element_type=F32)
+        + jnp.dot(low, mix_ref[0], preferred_element_type=F32)
+        + jnp.dot(high, mix_ref[1], preferred_element_type=F32)
     )
 
 
-def rows_mixed(value, left_ref):
+def rows_mixed(value, mix_ref):
     high, low = halves(value)
-    return jnp.dot(
-        left_ref[...], jnp.concatenate([high, low, high], 0), preferred_element_type=F32
+    return (
+        jnp.dot(mix_ref[0], high, preferred_element_type=F32)
+        + jnp.dot(mix_ref[0], low, preferred_element_type=F32)
+        + jnp.dot(mix_ref[1], high, preferred_element_type=F32)
     )
 
 
-def filtered(real, imag, mult_re, mult_im, left_ref, right_ref):
+def filtered(real, imag, mult_re, mult_im, mix_ref):
     width = real.shape[0]
-    mixed = columns_mixed(jnp.concatenate([real, imag], 0), right_ref)
-    real = rows_mixed(mixed[:width], left_ref)
-    imag = rows_mixed(mixed[width:], left_ref)
+    mixed = columns_mixed(jnp.concatenate([real, imag], 0), mix_ref)
+    real = rows_mixed(mixed[:width], mix_ref)
+    imag = rows_mixed(mixed[width:], mix_ref)
     if mult_im is None:
         real, imag = real * mult_re, imag * mult_re
     else:
         real, imag = real * mult_re - imag * mult_im, real * mult_im + imag * mult_re
-    real = rows_mixed(real, left_ref)
-    imag = rows_mixed(imag, left_ref)
-    mixed = columns_mixed(jnp.concatenate([real, imag], 0), right_ref)
+    real = rows_mixed(real, mix_ref)
+    imag = rows_mixed(imag, mix_ref)
+    mixed = columns_mixed(jnp.concatenate([real, imag], 0), mix_ref)
     return mixed[:width], mixed[width:]
 
 
@@ -95,19 +94,43 @@
 
 
 def kernel(
-    pair_ref, cutoff_ref, index_ref, target_ref, left_ref, right_ref, wave_ref, square_ref,
+    pair_ref, cutoff_ref, index_hbm, target_hbm, mix_hbm, wave_hbm,
     out_ref,
-    gathered_ref, field_ref, adjoint_ref, term_ref, inbox_ref, total_ref, part_ref,
+    target_ref, mix_ref, wave_ref, gathered_ref, field_ref, adjoint_ref, square_ref, term_ref, inbox_ref, total_ref, part_ref,
     own_send, relay_send, gather_recv, term_send, term_recv, sum_send, sum_recv,
-    part_send, part_recv, turn_sem,
+    part_send, part_recv, load_sem,
 ):
-    slabs, width = index_ref.shape[0], index_ref.shape[1]
+    slabs, width = index_hbm.shape[0], index_hbm.shape[1]
     slices = gathered_ref.shape[0]
-    members = target_ref.shape[0]
+    members = target_hbm.shape[0]
     levels, angles = lax.axis_size("depth"), lax.axis_size("angle")
     rows = width // angles
     place, spoke = lax.axis_index("depth"), lax.axis_index("angle")
     worker = place < members
+    pieces = 2 - angles % 2
+    piece = spoke % pieces
+    partner = spoke + 1 - 2 * piece if pieces == 2 else spoke
+
+    def load(number):
+        pairs = (
+            (mix_hbm, mix_ref),
+            (wave_hbm, wave_ref),
+            (target_hbm.at[lax.rem(place, members)], target_ref),
+        )
+        return pltpu.make_async_copy(*pairs[number], load_sem.at[slabs + number])
+
+    def load_slab(slab):
+        return pltpu.make_async_copy(
+            index_hbm.at[slab], gathered_ref.at[place * slabs + slab], load_sem.at[slab]
+        )
+
+    for slab in range(slabs):
+        load_slab(slab).start()
+
+    @pl.when(worker)
+    def _():
+        for number in range(3):
+            load(number).start()
 
     barrier = pltpu.get_barrier_semaphore()
     for step in range(1, levels):
@@ -118,7 +141,22 @@
         pl.semaphore_signal(
             barrier, device_id={"angle": lax.rem(spoke + step, angles)}, device_id_type=MESH
         )
-    pl.semaphore_wait(barrier, levels + angles - 2)
+    if pieces == 2:
+        @pl.when(worker)
+        def _():
+            for step in range(1, members):
+                pl.semaphore_signal(
+                    barrier,
+                    device_id={"depth": lax.rem(place + step, members), "angle": partner},
+                    device_id_type=MESH,
+                )
+            pl.semaphore_wait(barrier, levels + angles + members - 3)
+
+        @pl.when(jnp.logical_not(worker))
+        def _():
+            pl.semaphore_wait(barrier, levels + angles - 2)
+    else:
+        pl.semaphore_wait(barrier, levels + angles - 2)
 
     def remote(source, target, send, recv, device):
         return pltpu.make_async_remote_copy(
@@ -126,18 +164,47 @@
             device_id=device, device_id_type=MESH,
         )
 
+    tall = width // pieces
+
+    def piece_of(level, number):
+        return gathered_ref.at[level, pl.ds(pl.multiple_of(number * tall, tall), tall)]
+
     def own_copy(slab, step):
         level = place * slabs + slab
         return remote(
-            index_ref.at[slab], gathered_ref.at[level], own_send.at[slab, step],
-            gather_recv.at[level], {"depth": lax.rem(place + step, members)},
-        )
-
-    def relay_copy(level, step):
-        return remote(
-            gathered_ref.at[level], gathered_ref.at[level], relay_send.at[level, step],
-            gather_recv.at[level], {"depth": lax.rem(place + step, members)},
-        )
+            gathered_ref.at[level], gathered_ref.at[level], own_send.at[slab, step],
+            gather_recv.at[level, 0], {"depth": lax.rem(place + step, members)},
+        )
+
+    def own_wait(level):
+        remote(
+            gathered_ref.at[level], gathered_ref.at[level], relay_send.at[level, 0, 0],
+            gather_recv.at[level, 0], {"depth": lax.rem(place + 1, levels)},
+        ).wait_recv()
+
+    def entry_copy(slab):
+        level = place * slabs + slab
+        return remote(
+            piece_of(level, piece), piece_of(level, piece), own_send.at[slab, 0],
+            gather_recv.at[level, piece], {"depth": lax.rem(place, members)},
+        )
+
+    def relay_copy(level, step, across):
+        device = {"depth": lax.rem(place + step, members)}
+        if across:
+            device["angle"] = partner
+        return remote(
+            piece_of(level, piece), piece_of(level, piece),
+            relay_send.at[level, across, step], gather_recv.at[level, piece], device,
+        )
+
+    relays = [(step, across) for across in range(pieces) for step in range(members) if step + across]
+
+    def piece_wait(level, number):
+        remote(
+            piece_of(level, number), piece_of(level, number), relay_send.at[level, 0, 0],
+            gather_recv.at[level, number], {"depth": lax.rem(place + 1, levels)},
+        ).wait_recv()
 
     def term_copy(level):
         entry = (level // slabs) % members
@@ -167,22 +234,16 @@
 
     @pl.when(jnp.logical_not(worker))
     def _():
-        @pl.when(place > members)
-        def _():
-            pl.semaphore_wait(turn_sem, 1)
-
         for slab in range(slabs):
-            copy = own_copy(slab, 0)
-            copy.start()
-            copy.wait_send()
-
-        @pl.when(place < levels - 1)
-        def _():
-            pl.semaphore_signal(turn_sem, device_id={"depth": lax.rem(place + 1, levels)}, device_id_type=MESH)
+            load_slab(slab).wait()
+            entry_copy(slab).start()
 
         for slab in reversed(range(slabs)):
             sum_copy(place * slabs + slab).wait_recv()
             start_parts(slab)
+
+        for slab in range(slabs):
+            entry_copy(slab).wait_send()
 
     def work():
         kx, ky = pair_ref[place, 0], pair_ref[place, 1]
@@ -197,21 +258,33 @@
         )
         row_re, row_im = row_re * lead_re - row_im * lead_im, row_re * lead_im + row_im * lead_re
 
+        def frequency(index):
+            return jnp.where(index < width // 2, index, index - width)
+
         def relay(level):
             owner = level // slabs
 
             @pl.when((owner >= members) & (owner % members == place) & (level < slices))
             def _():
-                relay_copy(level, 0).wait_recv()
-                for step in range(1, members):
-                    relay_copy(level, step).start()
+                piece_wait(level, piece)
+                for step, across in relays:
+                    relay_copy(level, step, across).start()
 
         def ready(level):
             owner = level // slabs
 
-            @pl.when((owner != place) & ((owner < members) | (owner % members != place)))
-            def _():
-                relay_copy(level, 0).wait_recv()
+            @pl.when((owner != place) & (owner < members))
+            def _():
+                own_wait(level)
+
+            @pl.when((owner >= members) & (owner % members != place))
+            def _():
+                piece_wait(level, piece)
+
+            if pieces == 2:
+                @pl.when(owner >= members)
+                def _():
+                    piece_wait(level, 1 - piece)
 
         def screened(level, real, imag):
             screen_re, screen_im = sincos_small(screen_scale * gathered_ref[level])
@@ -220,20 +293,27 @@
 
         relay(0)
         relay(1)
+        relay(2)
         ready(0)
         screened(0, row_re * col_re - row_im * col_im, row_re * col_im + row_im * col_re)
 
         def forward(level, carry):
             real, imag = filtered(
                 field_ref[level - 1, 0], field_ref[level - 1, 1],
-                wave_ref[0], wave_ref[1], left_ref, right_ref,
+                wave_ref[0], wave_ref[1], mix_ref,
             )
-            relay(level + 1)
+            relay(level + 2)
             ready(level)
             screened(level, real, imag)
             return carry
 
+        for number in range(2):
+            load(number).wait()
         lax.fori_loop(1, slices, forward, 0)
+        load(2).wait()
+        freq_row = frequency(lax.broadcasted_iota(jnp.int32, (width, width), 0))
+        freq_col = frequency(lax.broadcasted_iota(jnp.int32, (width, width), 1))
+        square_ref[...] = (freq_row * freq_row + freq_col * freq_col).astype(F32)
         cutoff = cutoff_ref[0]
         limit = (cutoff * cutoff).astype(F32)
         adjoint_ref[0] = field_ref[slices - 1, 0]
@@ -242,9 +322,9 @@
         def through_pupil(turn, carry):
             pupil = (square_ref[...] <= limit).astype(F32)
             real, imag = filtered(
-                adjoint_ref[0], adjoint_ref[1], pupil, None, left_ref, right_ref
+                adjoint_ref[0], adjoint_ref[1], pupil, None, mix_ref
             )
-            misfit = 2.0 * (real * real + imag * imag - target_ref[place])
+            misfit = 2.0 * (real * real + imag * imag - target_ref[...])
             misfit = jnp.where(turn == 0, misfit, 1.0)
             adjoint_ref[0] = misfit * real
             adjoint_ref[1] = misfit * imag
@@ -293,7 +373,7 @@
             screen_re, screen_im = sincos_small(screen_scale * gathered_ref[level])
             real, imag = real * screen_re + imag * screen_im, imag * screen_re - real * screen_im
             real, imag = filtered(
-                real, imag, wave_ref[0], -wave_ref[1], left_ref, right_ref
+                real, imag, wave_ref[0], -wave_ref[1], mix_ref
             )
             adjoint_ref[0] = real
             adjoint_ref[1] = imag
@@ -307,10 +387,9 @@
     @pl.when(worker)
     def _():
         for slab in range(slabs):
+            load_slab(slab).wait()
             for step in range(1, members):
                 own_copy(slab, step).start()
-        for slab in range(slabs):
-            gathered_ref[place * slabs + slab] = index_ref[slab]
         work()
 
     for slab in reversed(range(slabs)):
@@ -336,8 +415,8 @@
 
             @pl.when((owner >= members) & (entry == place))
             def _():
-                for step in range(1, members):
-                    relay_copy(level, step).wait_send()
+                for step, across in relays:
+                    relay_copy(level, step, across).wait_send()
                 sum_copy(level).wait_send()
 
             @pl.when(entry != place)
@@ -354,38 +433,42 @@
     members = measured.shape[0]
     levels, angles = lax.axis_size("depth"), lax.axis_size("angle")
     slices = slabs * levels
-    left, right, wave, square = tables(width)
+    mix, wave = tables(width)
     smem = pl.BlockSpec(memory_space=pltpu.SMEM)
-    vmem = pl.BlockSpec(memory_space=pltpu.VMEM)
+    hbm = pl.BlockSpec(memory_space=pl.ANY)
     sem = pltpu.SemaphoreType.DMA
     return pl.pallas_call(
         kernel,
         out_shape=jax.ShapeDtypeStruct((slabs, width // angles, width), F32),
-        in_specs=[smem] * 2 + [vmem] * 6,
-        out_specs=vmem,
+        in_specs=[smem] * 2 + [hbm] * 4,
+        out_specs=pl.BlockSpec(memory_space=pltpu.VMEM),
         scratch_shapes=[
+            pltpu.VMEM((width, width), F32),
+            pltpu.VMEM((2, width, width), BF16),
+            pltpu.VMEM((2, width, width), F32),
             pltpu.VMEM((slices, width, width), F32),
             pltpu.VMEM((slices, 2, width, width), F32),
             pltpu.VMEM((2, width, width), F32),
+            pltpu.VMEM((width, width), F32),
             pltpu.VMEM((slices, width, width), F32),
             pltpu.VMEM((slices, members, width, width), F32),
             pltpu.VMEM((slabs, width, width), F32),
             pltpu.VMEM((slabs, angles, width // angles, width), F32),
             sem((slabs, members)),
-            sem((slices, members)),
-            sem((slices,)),
+            sem((slices, 2, members)),
+            sem((slices, 2)),
             sem((slices,)),
             sem((slices, members)),
             sem((slices,)),
             sem((slabs,)),
             sem((slabs, angles)),
             sem((slabs, angles)),
-            pltpu.SemaphoreType.REGULAR,
+            sem((slabs + 3,)),
         ],
         compiler_params=pltpu.CompilerParams(
             collective_id=0, has_side_effects=True, vmem_limit_bytes=60 * 2**20
         ),
-    )(angle_index, cutoff, index_change, measured, left, right, wave, square)
+    )(angle_index, cutoff, index_change, measured, mix, wave)
 
 
 def solution(mesh):

time: 54.2 us -> 55.1 us (1.017)
  Pallas kernels: 51.8 us -> 52.7 us
    pallas_call x1, Pallas kernels: 51.8 us -> 52.7 us  [body(): pl.pallas_call(kernel, out_shape=jax.ShapeDtypeStruct((slabs, width // an...]
where the time goes in v3:
time: 55.1 us; the launch traced here: 55 us
  Pallas kernels  52.7 us (96%)
  local copies, waits for them, and re-layouts  1.57 us (3%)
  between operations  0.66 us (1%)
    pallas_call x1, Pallas kernels, body(): pl.pallas_call(kernel, out_shape=jax.ShapeDtypeStruct((slabs, width // an...  52.7 us
    unnamed x1, local copies, waits for them, and re-layouts  1.57 us

profile of v3, /device:TPU:0, one launch (start us, length us, event | category | flops | bytes accessed | tf_op | source)
XLA Modules:
  0.0 55.0 jit_solution(2429703085370507893)
XLA Ops:
  0.7 52.7 %shard_map.64 = f32[2,64,256]{2,1,0:T(8,128)} custom-call(s32[2,2]{1,0:T(2,128)} %pair_ref.1, s32[1]{0:T(128)S(6)} %copy.8.cutoff_ref, f32[2,256,256]{2,1,0:T(8,128)} %index_hbm.1, f32[2,256,256]{2,1,0:T(8,128)} %target_hbm.1, bf16[2,256,256]{2,1,0:T(8,128)(2,1)} %constant.4.clone.mix_hbm, f32[2,256,256]{2,1,0:T(8,128)} %constant.5.clone.wave_hbm), custom_call_target="tpu_custom_call" | custom-call | tf_op jit(solution)/shard_map/pallas_call | solution.py:440
  53.4 1.6 %copy.9 = f32[2,64,256]{2,1,0:T(8,128)} copy(f32[2,64,256]{2,1,0:T(8,128)} %shard_map.64) | data formatting | bytes 262144

commit v4 on v3

--- a/solution.py
+++ b/solution.py
@@ -98,7 +98,7 @@
     out_ref,
     target_ref, mix_ref, wave_ref, gathered_ref, field_ref, adjoint_ref, square_ref, term_ref, inbox_ref, total_ref, part_ref,
     own_send, relay_send, gather_recv, term_send, term_recv, sum_send, sum_recv,
-    part_send, part_recv, load_sem,
+    part_send, part_recv, load_sem, turn_sem,
 ):
     slabs, width = index_hbm.shape[0], index_hbm.shape[1]
     slices = gathered_ref.shape[0]
@@ -141,22 +141,7 @@
         pl.semaphore_signal(
             barrier, device_id={"angle": lax.rem(spoke + step, angles)}, device_id_type=MESH
         )
-    if pieces == 2:
-        @pl.when(worker)
-        def _():
-            for step in range(1, members):
-                pl.semaphore_signal(
-                    barrier,
-                    device_id={"depth": lax.rem(place + step, members), "angle": partner},
-                    device_id_type=MESH,
-                )
-            pl.semaphore_wait(barrier, levels + angles + members - 3)
-
-        @pl.when(jnp.logical_not(worker))
-        def _():
-            pl.semaphore_wait(barrier, levels + angles - 2)
-    else:
-        pl.semaphore_wait(barrier, levels + angles - 2)
+    pl.semaphore_wait(barrier, levels + angles - 2)
 
     def remote(source, target, send, recv, device):
         return pltpu.make_async_remote_copy(
@@ -189,16 +174,18 @@
             gather_recv.at[level, piece], {"depth": lax.rem(place, members)},
         )
 
-    def relay_copy(level, step, across):
-        device = {"depth": lax.rem(place + step, members)}
-        if across:
-            device["angle"] = partner
+    def relay_copy(level, number, step):
+        return remote(
+            piece_of(level, number), piece_of(level, number),
+            relay_send.at[level, number, step], gather_recv.at[level, number],
+            {"depth": lax.rem(place + step, members)},
+        )
+
+    def cross_copy(level):
         return remote(
             piece_of(level, piece), piece_of(level, piece),
-            relay_send.at[level, across, step], gather_recv.at[level, piece], device,
-        )
-
-    relays = [(step, across) for across in range(pieces) for step in range(members) if step + across]
+            relay_send.at[level, 0, 0], gather_recv.at[level, piece], {"angle": partner},
+        )
 
     def piece_wait(level, number):
         remote(
@@ -236,14 +223,25 @@
     def _():
         for slab in range(slabs):
             load_slab(slab).wait()
+
+        @pl.when(place > members)
+        def _():
+            pl.semaphore_wait(turn_sem, 1)
+
+        for slab in range(slabs):
             entry_copy(slab).start()
+        for slab in range(slabs):
+            entry_copy(slab).wait_send()
+
+        @pl.when(place < levels - 1)
+        def _():
+            pl.semaphore_signal(
+                turn_sem, device_id={"depth": lax.rem(place + 1, levels)}, device_id_type=MESH
+            )
 
         for slab in reversed(range(slabs)):
             sum_copy(place * slabs + slab).wait_recv()
             start_parts(slab)
-
-        for slab in range(slabs):
-            entry_copy(slab).wait_send()
 
     def work():
         kx, ky = pair_ref[place, 0], pair_ref[place, 1]
@@ -267,8 +265,20 @@
             @pl.when((owner >= members) & (owner % members == place) & (level < slices))
             def _():
                 piece_wait(level, piece)
-                for step, across in relays:
-                    relay_copy(level, step, across).start()
+                if pieces == 2:
+                    cross_copy(level).start()
+                for step in range(1, members):
+                    relay_copy(level, piece, step).start()
+
+        def second_relay(level):
+            owner = level // slabs
+
+            if pieces == 2:
+                @pl.when((owner >= members) & (owner % members == place) & (level < slices))
+                def _():
+                    piece_wait(level, 1 - piece)
+                    for step in range(1, members):
+                        relay_copy(level, 1 - piece, step).start()
 
         def ready(level):
             owner = level // slabs
@@ -279,12 +289,8 @@
 
             @pl.when((owner >= members) & (owner % members != place))
             def _():
-                piece_wait(level, piece)
-
-            if pieces == 2:
-                @pl.when(owner >= members)
-                def _():
-                    piece_wait(level, 1 - piece)
+                for number in range(pieces):
+                    piece_wait(level, number)
 
         def screened(level, real, imag):
             screen_re, screen_im = sincos_small(screen_scale * gathered_ref[level])
@@ -294,6 +300,8 @@
         relay(0)
         relay(1)
         relay(2)
+        second_relay(0)
+        second_relay(1)
         ready(0)
         screened(0, row_re * col_re - row_im * col_im, row_re * col_im + row_im * col_re)
 
@@ -303,6 +311,7 @@
                 wave_ref[0], wave_ref[1], mix_ref,
             )
             relay(level + 2)
+            second_relay(level + 1)
             ready(level)
             screened(level, real, imag)
             return carry
@@ -415,8 +424,11 @@
 
             @pl.when((owner >= members) & (entry == place))
             def _():
-                for step, across in relays:
-                    relay_copy(level, step, across).wait_send()
+                if pieces == 2:
+                    cross_copy(level).wait_send()
+                for step in range(1, members):
+                    for number in range(pieces):
+                        relay_copy(level, number, step).wait_send()
                 sum_copy(level).wait_send()
 
             @pl.when(entry != place)
@@ -464,6 +476,7 @@
             sem((slabs, angles)),
             sem((slabs, angles)),
             sem((slabs + 3,)),
+            pltpu.SemaphoreType.REGULAR,
         ],
         compiler_params=pltpu.CompilerParams(
             collective_id=0, has_side_effects=True, vmem_limit_bytes=60 * 2**20

time: 55.1 us -> 51.8 us (0.940)
  Pallas kernels: 52.7 us -> 49.5 us
    pallas_call x1, Pallas kernels: 52.7 us -> 49.5 us  [body(): pl.pallas_call(kernel, out_shape=jax.ShapeDtypeStruct((slabs, width // an...]
where the time goes in v4:
time: 51.8 us; the launch traced here: 51.7 us
  Pallas kernels  49.5 us (96%)
  local copies, waits for them, and re-layouts  1.57 us (3%)
  between operations  0.66 us (1%)
    pallas_call x1, Pallas kernels, body(): pl.pallas_call(kernel, out_shape=jax.ShapeDtypeStruct((slabs, width // an...  49.5 us
    unnamed x1, local copies, waits for them, and re-layouts  1.57 us

profile of v4, /device:TPU:0, one launch (start us, length us, event | category | flops | bytes accessed | tf_op | source)
XLA Modules:
  0.0 51.7 jit_solution(13660117230283223808)
XLA Ops:
  0.7 49.5 %shard_map.64 = f32[2,64,256]{2,1,0:T(8,128)} custom-call(s32[2,2]{1,0:T(2,128)} %pair_ref.1, s32[1]{0:T(128)S(6)} %copy.8.cutoff_ref, f32[2,256,256]{2,1,0:T(8,128)} %index_hbm.1, f32[2,256,256]{2,1,0:T(8,128)} %target_hbm.1, bf16[2,256,256]{2,1,0:T(8,128)(2,1)} %constant.4.clone.mix_hbm, f32[2,256,256]{2,1,0:T(8,128)} %constant.5.clone.wave_hbm), custom_call_target="tpu_custom_call" | custom-call | tf_op jit(solution)/shard_map/pallas_call | solution.py:452
  50.1 1.6 %copy.9 = f32[2,64,256]{2,1,0:T(8,128)} copy(f32[2,64,256]{2,1,0:T(8,128)} %shard_map.64) | data formatting | bytes 262144

commit v5 on v4

--- a/solution.py
+++ b/solution.py
@@ -96,9 +96,9 @@
 def kernel(
     pair_ref, cutoff_ref, index_hbm, target_hbm, mix_hbm, wave_hbm,
     out_ref,
-    target_ref, mix_ref, wave_ref, gathered_ref, field_ref, adjoint_ref, square_ref, term_ref, inbox_ref, total_ref, part_ref,
+    target_ref, mix_ref, wave_ref, gathered_ref, field_ref, adjoint_ref, square_ref, term_ref, inbox_ref, total_ref, part_ref, mate_ref,
     own_send, relay_send, gather_recv, term_send, term_recv, sum_send, sum_recv,
-    part_send, part_recv, load_sem, turn_sem,
+    part_send, part_recv, pair_send, pair_recv, load_sem, turn_sem,
 ):
     slabs, width = index_hbm.shape[0], index_hbm.shape[1]
     slices = gathered_ref.shape[0]
@@ -207,16 +207,36 @@
             sum_recv.at[level % slabs], {"depth": level // slabs},
         )
 
+    hops = angles // pieces
+
+    def block_of(slab, goal):
+        return total_ref.at[slab, pl.ds(pl.multiple_of(goal * rows, rows), rows)]
+
+    def pair_copy(slab, number):
+        return remote(
+            block_of(slab, 2 * number + 1 - piece), mate_ref.at[slab, number],
+            pair_send.at[slab, number], pair_recv.at[slab, number], {"angle": partner},
+        )
+
     def part_copy(slab, step):
-        goal = lax.rem(spoke + step, angles)
-        return remote(
-            total_ref.at[slab, pl.ds(pl.multiple_of(goal * rows, rows), rows)],
-            part_ref.at[slab, step], part_send.at[slab, step], part_recv.at[slab, step],
-            {"angle": goal},
-        )
+        goal = lax.rem(spoke + pieces * step, angles)
+        return remote(
+            block_of(slab, goal), part_ref.at[slab, step],
+            part_send.at[slab, step], part_recv.at[slab, step], {"angle": goal},
+        )
+
+    def start_pair(slab):
+        if pieces == 2:
+            for number in range(hops):
+                pair_copy(slab, number).start()
 
     def start_parts(slab):
-        for step in range(1, angles):
+        if pieces == 2:
+            for number in range(hops):
+                pair_copy(slab, number).wait_recv()
+                block = block_of(slab, 2 * number + piece)
+                block[...] += mate_ref[slab, number]
+        for step in range(1, hops):
             part_copy(slab, step).start()
 
     @pl.when(jnp.logical_not(worker))
@@ -241,6 +261,7 @@
 
         for slab in reversed(range(slabs)):
             sum_copy(place * slabs + slab).wait_recv()
+            start_pair(slab)
             start_parts(slab)
 
     def work():
@@ -369,12 +390,17 @@
                 @pl.when(owner == place)
                 def _():
                     total_ref[level % slabs] = value
-                    start_parts(level % slabs)
+                    start_pair(level % slabs)
 
                 @pl.when(owner != place)
                 def _():
                     term_ref[level] = value
                     sum_copy(level).start()
+
+        def parts_on(level):
+            @pl.when((level // slabs == place) & (level < slices))
+            def _():
+                start_parts(level % slabs)
 
         def backward(step, carry):
             level = slices - 1 - step
@@ -387,11 +413,14 @@
             adjoint_ref[0] = real
             adjoint_ref[1] = imag
             pass_on(level)
+            parts_on(level + 1)
             return carry
 
         lax.fori_loop(0, slices - 1, backward, 0)
         with_term(0)
         pass_on(0)
+        parts_on(1)
+        parts_on(0)
 
     @pl.when(worker)
     def _():
@@ -403,14 +432,17 @@
 
     for slab in reversed(range(slabs)):
         value = total_ref[slab, pl.ds(pl.multiple_of(spoke * rows, rows), rows)]
-        for step in range(1, angles):
+        for step in range(1, hops):
             part_copy(slab, step).wait_recv()
             value = value + part_ref[slab, step]
         out_ref[slab] = value
 
     for slab in range(slabs):
-        for step in range(1, angles):
+        for step in range(1, hops):
             part_copy(slab, step).wait_send()
+        if pieces == 2:
+            for number in range(hops):
+                pair_copy(slab, number).wait_send()
 
     @pl.when(worker)
     def _():
@@ -466,6 +498,7 @@
             pltpu.VMEM((slices, members, width, width), F32),
             pltpu.VMEM((slabs, width, width), F32),
             pltpu.VMEM((slabs, angles, width // angles, width), F32),
+            pltpu.VMEM((slabs, angles, width // angles, width), F32),
             sem((slabs, members)),
             sem((slices, 2, members)),
             sem((slices, 2)),
@@ -475,6 +508,8 @@
             sem((slabs,)),
             sem((slabs, angles)),
             sem((slabs, angles)),
+            sem((slabs, angles)),
+            sem((slabs, angles)),
             sem((slabs + 3,)),
             pltpu.SemaphoreType.REGULAR,
         ],

time: 51.8 us -> 53.2 us (1.027)
  Pallas kernels: 49.5 us -> 50.8 us
    pallas_call x1, Pallas kernels: 49.5 us -> 50.8 us  [body(): pl.pallas_call(kernel, out_shape=jax.ShapeDtypeStruct((slabs, width // an...]
where the time goes in v5:
time: 53.2 us; the launch traced here: 53.1 us
  Pallas kernels  50.8 us (95%)
  local copies, waits for them, and re-layouts  1.57 us (3%)
  between operations  0.66 us (1%)
    pallas_call x1, Pallas kernels, body(): pl.pallas_call(kernel, out_shape=jax.ShapeDtypeStruct((slabs, width // an...  50.8 us
    unnamed x1, local copies, waits for them, and re-layouts  1.57 us

profile of v5, /device:TPU:0, one launch (start us, length us, event | category | flops | bytes accessed | tf_op | source)
XLA Modules:
  0.0 53.1 jit_solution(3695365812418174271)
XLA Ops:
  0.7 50.8 %shard_map.64 = f32[2,64,256]{2,1,0:T(8,128)} custom-call(s32[2,2]{1,0:T(2,128)} %pair_ref.1, s32[1]{0:T(128)S(6)} %copy.8.cutoff_ref, f32[2,256,256]{2,1,0:T(8,128)} %index_hbm.1, f32[2,256,256]{2,1,0:T(8,128)} %target_hbm.1, bf16[2,256,256]{2,1,0:T(8,128)(2,1)} %constant.4.clone.mix_hbm, f32[2,256,256]{2,1,0:T(8,128)} %constant.5.clone.wave_hbm), custom_call_target="tpu_custom_call" | custom-call | tf_op jit(solution)/shard_map/pallas_call | solution.py:484
  51.5 1.6 %copy.9 = f32[2,64,256]{2,1,0:T(8,128)} copy(f32[2,64,256]{2,1,0:T(8,128)} %shard_map.64) | data formatting | bytes 262144

commit v6 on v4

--- a/solution.py
+++ b/solution.py
@@ -294,6 +294,8 @@
 
         def screened(level, real, imag):
             screen_re, screen_im = sincos_small(screen_scale * gathered_ref[level])
+            inbox_ref[level, 0] = screen_re
+            term_ref[level] = screen_im
             field_ref[level, 0] = real * screen_re - imag * screen_im
             field_ref[level, 1] = real * screen_im + imag * screen_re
 
@@ -378,8 +380,8 @@
 
         def backward(step, carry):
             level = slices - 1 - step
+            screen_re, screen_im = inbox_ref[level, 0], term_ref[level]
             real, imag = with_term(level)
-            screen_re, screen_im = sincos_small(screen_scale * gathered_ref[level])
             real, imag = real * screen_re + imag * screen_im, imag * screen_re - real * screen_im
             real, imag = filtered(
                 real, imag, wave_ref[0], -wave_ref[1], mix_ref

time: 51.8 us -> 51.5 us (level)
  no operation moved by 1% of the time
where the time goes in v6:
time: 51.5 us; the launch traced here: 51.3 us
  Pallas kernels  49.1 us (95%)
  local copies, waits for them, and re-layouts  1.57 us (3%)
  between operations  0.66 us (1%)
    pallas_call x1, Pallas kernels, body(): pl.pallas_call(kernel, out_shape=jax.ShapeDtypeStruct((slabs, width // an...  49.1 us
    unnamed x1, local copies, waits for them, and re-layouts  1.57 us

profile of v6, /device:TPU:0, one launch (start us, length us, event | category | flops | bytes accessed | tf_op | source)
XLA Modules:
  0.0 51.3 jit_solution(13593976863145395593)
XLA Ops:
  0.7 49.1 %shard_map.64 = f32[2,64,256]{2,1,0:T(8,128)} custom-call(s32[2,2]{1,0:T(2,128)} %pair_ref.1, s32[1]{0:T(128)S(6)} %copy.8.cutoff_ref, f32[2,256,256]{2,1,0:T(8,128)} %index_hbm.1, f32[2,256,256]{2,1,0:T(8,128)} %target_hbm.1, bf16[2,256,256]{2,1,0:T(8,128)(2,1)} %constant.4.clone.mix_hbm, f32[2,256,256]{2,1,0:T(8,128)} %constant.5.clone.wave_hbm), custom_call_target="tpu_custom_call" | custom-call | tf_op jit(solution)/shard_map/pallas_call | solution.py:454
  49.8 1.6 %copy.9 = f32[2,64,256]{2,1,0:T(8,128)} copy(f32[2,64,256]{2,1,0:T(8,128)} %shard_map.64) | data formatting | bytes 262144
